TPU v7x, 1024 devices: a whole 8x8x8 slice. The times are simulated.
1024 devices in a mesh: expert: 64 (over y, z), hidden: 16 (over x, core).
Axes of the slice: x: 8, y: 8, z: 8, core: 2. Of those that a mesh axis runs over, the one named last changes fastest.
Arguments:
- tokens: bfloat16 [1024, 4096], P('expert', 'hidden'), may hold values from -6 to 6
- probs: float32 [1024, 8], P('expert'), may hold values from 0.05 to 0.6
- expert_ids: int32 [1024, 8], P('expert'), may hold values from 0 to 63, all different within a row; in each aligned block of 16 rows (0 to 15, 16 to 31, ...) at most 4 rows name the same one
- gate_weight: bfloat16 [64, 2048, 4096], P('expert', 'hidden'), may hold values from -0.09375 to 0.09375
- up_weight: bfloat16 [64, 2048, 4096], P('expert', 'hidden'), may hold values from -0.09375 to 0.09375
- down_weight: bfloat16 [64, 2048, 4096], P('expert', 'hidden'), may hold values from -0.125 to 0.125
- cotangent: bfloat16 [1024, 4096], P('expert', 'hidden'), may hold values from -6 to 6
Outputs:
- mixed: bfloat16 [1024, 4096], P('expert', 'hidden')
- grad_tokens: bfloat16 [1024, 4096], P('expert', 'hidden')
Inputs may be any that keep to these rules, and one draw needn't show every extreme that they name: `expert_ids`: each row names 8 different experts. Within the 16 rows of one group no expert is named more than 4 times, and in every draw some expert is named exactly 4 times by some group.
All inputs are finite; a program needn't handle non-finite values.
Results may differ from a plain program's by a relative error of at most 0.024.
Values may be sent and summed in bfloat16 or wider, within the bound.
A program may use at most 32 MiB of HBM per device.

v0:
```python
import jax
import jax.numpy as jnp
from jax import lax
from jax.sharding import PartitionSpec as P


def routing(expert_ids, probs, groups):
    tok_rows, top_k = expert_ids.shape
    capacity = min(tok_rows, max(2, 2 * tok_rows * top_k // groups))
    flat_ids = expert_ids.reshape(-1)
    onehot = (flat_ids[:, None] == jnp.arange(groups, dtype=jnp.int32)[None, :]).astype(jnp.int32)
    earlier = jnp.cumsum(onehot, axis=0) - onehot
    slot_index = jnp.sum(earlier * onehot, axis=1)
    position = flat_ids * capacity + slot_index
    select = (position[:, None] == jnp.arange(groups * capacity, dtype=jnp.int32)[None, :]).astype(
        jnp.float32
    )
    select = select.reshape(tok_rows, top_k, groups * capacity)
    member = jnp.sum(select, axis=1)
    slot_weight = jnp.sum(jnp.sum(select * probs[:, :, None], axis=1), axis=0)
    return (capacity, member.astype(jnp.bfloat16), slot_weight, position.reshape(tok_rows, top_k))


def shards(tokens, probs, expert_ids, gate_weight, up_weight, down_weight, cotangent):
    groups = lax.axis_size("expert")
    capacity, member, slot_weight, position = routing(expert_ids, probs, groups)
    placing = member.T
    w_gate = gate_weight[0]
    w_up = up_weight[0]
    w_down = down_weight[0]

    def place_rows(token_rows, scale):
        placed = jnp.dot(placing, token_rows, preferred_element_type=jnp.float32)
        if scale:
            placed = placed * slot_weight[:, None]
        return placed.astype(jnp.bfloat16)

    def combine(returned, scale):
        picked = returned[position].astype(jnp.float32)
        if scale:
            picked = picked * probs[:, :, None]
        return jnp.sum(picked, axis=1)

    def dispatch_slices(token_rows, scale):
        send_rows = place_rows(token_rows, scale)
        arrived = lax.all_to_all(
            send_rows.reshape(groups, capacity, send_rows.shape[1]),
            "expert",
            split_axis=0,
            concat_axis=0,
            tiled=True,
        )
        arrived = arrived.reshape(groups * capacity, send_rows.shape[1])
        return lax.all_gather(arrived, "hidden", axis=1, tiled=True)

    def collect_slices(partial_value, scale):
        term = lax.optimization_barrier(partial_value.astype(jnp.bfloat16)).astype(jnp.float32)
        summed = lax.psum_scatter(
            term.astype(jnp.bfloat16), "hidden", scatter_dimension=1, tiled=True
        ).astype(jnp.float32)
        width = summed.shape[1]
        returned = lax.all_to_all(
            summed.reshape(groups, capacity, width).astype(jnp.bfloat16),
            "expert",
            split_axis=0,
            concat_axis=0,
            tiled=True,
        ).astype(jnp.float32)
        returned = returned.reshape(groups * capacity, width)
        return combine(returned, scale)

    dispatch, collect = (dispatch_slices, collect_slices)
    contract = (((1,), (1,)), ((), ()))
    rows_in = dispatch(tokens, False)
    gate = lax.dot_general(rows_in, w_gate, contract, preferred_element_type=jnp.float32)
    upper = lax.dot_general(rows_in, w_up, contract, preferred_element_type=jnp.float32)
    hidden = (jax.nn.silu(gate) * upper).astype(jnp.bfloat16)
    partial_out = jnp.dot(hidden, w_down, preferred_element_type=jnp.float32)
    mixed = collect(partial_out, True).astype(jnp.bfloat16)
    scaled = dispatch(cotangent, True)
    grad_hidden = lax.dot_general(scaled, w_down, contract, preferred_element_type=jnp.float32)
    sigma = jax.nn.sigmoid(gate)
    grad_gate = (grad_hidden * upper * sigma * (1.0 + gate * (1.0 - sigma))).astype(jnp.bfloat16)
    grad_up = (grad_hidden * gate * sigma).astype(jnp.bfloat16)
    partial_grad = jnp.dot(grad_gate, w_gate, preferred_element_type=jnp.float32)
    partial_grad = partial_grad + jnp.dot(grad_up, w_up, preferred_element_type=jnp.float32)
    grad_tokens = collect(partial_grad, False).astype(jnp.bfloat16)
    return (mixed, grad_tokens)


def solution(mesh):
    placed = (
        P("expert", "hidden"),
        P("expert", None),
        P("expert", None),
        P("expert", "hidden", None),
        P("expert", "hidden", None),
        P("expert", "hidden", None),
        P("expert", "hidden"),
    )
    return jax.shard_map(
        shards,
        mesh=mesh,
        in_specs=placed,
        out_specs=(P("expert", "hidden"), P("expert", "hidden")),
        check_vma=False,
    )
```

profile of v0, /device:TPU:16, one launch (start us, length us, event | category | flops | bytes accessed | tf_op | source)
XLA Modules:
  0.0 303.4 jit_solution(10453938823580128862)
XLA Ops:
  7.2 0.9 copy.14
  8.1 0.8 copy.12
  8.9 0.1 eq.29
  9.0 0.1 fusion.16
  9.1 0.2 reduce_window_sum.11
  9.2 0.2 select_reduce_fusion.1
  9.5 0.1 select_reduce_fusion
  9.7 0.9 convolution_convert_fusion.1
  10.6 34.7 %all_to_all.20 = bf16[64,4,256]{2,1,0:T(4,128)(2,1)S(1)} all-to-all(bf16[64,4,256]{2,1,0:T(4,128)(2,1)S(1)} %reshape.55), channel_id=1, replica_groups=mesh['expert'=64,'hidden'=16] {'expert'}, dimensions={0} | all-to-all | bytes 262144 | tf_op jit(solution)/shard_map/all_to_all | solution.py:46
  45.4 0.7 reshape.56
  46.1 0.9 fusion.1
  47.1 16.9 %all_to_all.21 = bf16[64,4,256]{2,1,0:T(4,128)(2,1)S(1)} all-to-all(bf16[64,4,256]{2,1,0:T(4,128)(2,1)S(1)} %reshape.59), channel_id=1, replica_groups=mesh['expert'=64,'hidden'=16] {'expert'}, dimensions={0} | all-to-all | bytes 262144 | tf_op jit(solution)/shard_map/all_to_all | solution.py:46
  64.0 0.7 reshape.60
  64.7 19.7 %all-gather.3.cloned.1.call-done = bf16[256,4096]{1,0:T(8,128)(2,1)} async-done(((bf16[256,256]{1,0:T(8,128)(2,1)}), bf16[256,4096]{1,0:T(8,128)(2,1)}) %all-gather.3.cloned.1.call-update) | async-done | bytes 2097168 | tf_op jit(solution)/shard_map/all_gather | solution.py:54
  84.5 2.4 fusion.10
  86.9 0.7 fusion.6
  87.7 2.0 convolution_convert_fusion
  89.7 43.5 %all-gather.5.cloned.1.call-done = bf16[256,4096]{1,0:T(8,128)(2,1)} async-done(((bf16[256,256]{1,0:T(8,128)(2,1)}), bf16[256,4096]{1,0:T(8,128)(2,1)}) %all-gather.5.cloned.1.call-update) | async-done | bytes 2097168 | tf_op jit(solution)/shard_map/all_gather | solution.py:54
  133.2 2.3 fusion.2
  135.5 0.7 fusion.8
  136.2 2.1 fusion
  138.3 62.6 %reduce-scatter.3.cloned.1.call-done = bf16[256,256]{1,0:T(8,128)(2,1)} async-done(((bf16[256,4096]{1,0:T(8,128)(2,1)}), bf16[256,256]{1,0:T(8,128)(2,1)}) %reduce-scatter.3.cloned.1.call-update) | async-done | bytes 131088 | tf_op jit(solution)/shard_map/reduce_scatter | solution.py:58
  200.9 1.6 convert_element_type.59
  202.5 14.2 %all-to-all-start.1 = ((bf16[64,4,256]{2,1,0:T(4,128)(2,1)}), bf16[64,4,256]{2,1,0:T(4,128)(2,1)S(1)}, u32[]{:S(2)}, u32[]{:S(2)}) async-start(bf16[64,4,256]{2,1,0:T(4,128)(2,1)} %convert_element_type.59), calls=%async_computation.2 | async-start | bytes 262144 | tf_op jit(solution)/shard_map/all_to_all | solution.py:62
  216.7 51.3 %reduce-scatter.5.cloned.1.call-done = bf16[256,256]{1,0:T(8,128)(2,1)} async-done(((bf16[256,4096]{1,0:T(8,128)(2,1)}), bf16[256,256]{1,0:T(8,128)(2,1)}) %reduce-scatter.5.cloned.1.call-update) | async-done | bytes 131088 | tf_op jit(solution)/shard_map/reduce_scatter | solution.py:58
  268.0 1.6 convert_element_type.65
  269.6 14.1 %all-to-all-start.3 = ((bf16[64,4,256]{2,1,0:T(4,128)(2,1)}), bf16[64,4,256]{2,1,0:T(4,128)(2,1)S(1)}, u32[]{:S(2)}, u32[]{:S(2)}) async-start(bf16[64,4,256]{2,1,0:T(4,128)(2,1)} %convert_element_type.65), calls=%async_computation.5 | async-start | bytes 262144 | tf_op jit(solution)/shard_map/all_to_all | solution.py:62
  283.9 0.8 gather_fusion
  284.6 0.7 fusion.12
  285.3 10.1 %all-to-all-done.3 = bf16[64,4,256]{2,1,0:T(4,128)(2,1)S(1)} async-done(((bf16[64,4,256]{2,1,0:T(4,128)(2,1)}), bf16[64,4,256]{2,1,0:T(4,128)(2,1)S(1)}, u32[]{:S(2)}, u32[]{:S(2)}) %all-to-all-start.3) | async-done | bytes 131104 | tf_op jit(solution)/shard_map/all_to_all | solution.py:62
  295.5 0.8 gather_fusion.1
  296.2 0.6 bitcast_reduce_fusion
  (25 shorter events, 0.6 us)
Async XLA Ops:
  7.2 80.5 %copy-start = (bf16[1,128,4096]{2,1,0:T(8,128)(2,1)S(1)}, bf16[1,128,4096]{2,1,0:T(8,128)(2,1)}, u32[]{:S(2)}) copy-start(bf16[1,128,4096]{2,1,0:T(8,128)(2,1)} %param.12) | copy-start | bytes 3145732
  7.2 77.3 %copy-start.2 = (bf16[1,128,4096]{2,1,0:T(8,128)(2,1)S(1)}, bf16[1,128,4096]{2,1,0:T(8,128)(2,1)}, u32[]{:S(2)}) copy-start(bf16[1,128,4096]{2,1,0:T(8,128)(2,1)} %param.10) | copy-start | bytes 3145732
  7.2 77.3 %all-gather.3.cloned.1.call-start = ((), (), s32[]{:S(2)}) async-start(), calls=%async_computation.6 | async-start | bytes 2228224 | tf_op jit(solution)/shard_map/all_gather | solution.py:54
  46.1 87.1 %all-gather.5.cloned.1.call-start = ((), (), s32[]{:S(2)}) async-start(), calls=%async_computation.8 | async-start | bytes 2228224 | tf_op jit(solution)/shard_map/all_gather | solution.py:54
  47.0 39.9 %copy-start.3 = (bf16[1,128,4096]{2,1,0:T(8,128)(2,1)S(1)}, bf16[1,128,4096]{2,1,0:T(8,128)(2,1)}, u32[]{:S(2)}) copy-start(bf16[1,128,4096]{2,1,0:T(8,128)(2,1)} %param.11) | copy-start | bytes 3145732
  64.7 136.2 %reduce-scatter.3.cloned.1.call-start = ((), (), s32[]{:S(2)}) async-start(), calls=%async_computation.7 | async-start | bytes 2228224 | tf_op jit(solution)/shard_map/reduce_scatter | solution.py:58
  84.5 2.5 copy-start.1
  89.7 178.4 %reduce-scatter.5.cloned.1.call-start = ((), (), s32[]{:S(2)}) async-start(), calls=%async_computation.9 | async-start | bytes 2228224 | tf_op jit(solution)/shard_map/reduce_scatter | solution.py:58
  202.5 67.1 %all-to-all-start.1 = ((bf16[64,4,256]{2,1,0:T(4,128)(2,1)}), bf16[64,4,256]{2,1,0:T(4,128)(2,1)S(1)}, u32[]{:S(2)}, u32[]{:S(2)}) async-start(bf16[64,4,256]{2,1,0:T(4,128)(2,1)} %convert_element_type.59), calls=%async_computation.2 | async-start | bytes 262144 | tf_op jit(solution)/shard_map/all_to_all | solution.py:62
  269.6 25.8 %all-to-all-start.3 = ((bf16[64,4,256]{2,1,0:T(4,128)(2,1)}), bf16[64,4,256]{2,1,0:T(4,128)(2,1)S(1)}, u32[]{:S(2)}, u32[]{:S(2)}) async-start(bf16[64,4,256]{2,1,0:T(4,128)(2,1)} %convert_element_type.65), calls=%async_computation.5 | async-start | bytes 262144 | tf_op jit(solution)/shard_map/all_to_all | solution.py:62
Sparse Core Ops, SparseCore 0:
  46.2 38.2 all-gather.2
  87.1 46.0 all-gather.4
  136.6 64.2 reduce-scatter.2
  204.2 63.8 reduce-scatter.4
where the time goes:
time: 304 us; the launch traced here: 303 us
  waiting for transfers between devices  187 us (62%)
  blocking collectives  51.6 us (17%)
  starting transfers between devices  28.4 us (9%)
  between operations  13.9 us (5%)
  matrix products  12.1 us (4%)
  local copies, waits for them, and re-layouts  8.07 us (3%)
    reduce_scatter x2, waiting for transfers between devices, collect_slices(): lax.psum_scatter(term.astype(jnp.bfloat16), 'hidden', scatter_dimension=1...  114 us
    all_gather x2, waiting for transfers between devices, dispatch_slices(): return lax.all_gather(arrived, 'hidden', axis=1, tiled=True)  63.2 us
    all_to_all x2, blocking collectives, dispatch_slices(): lax.all_to_all(send_rows.reshape(groups, capacity, send_rows.shape[1]), '...  51.6 us
    all_to_all x2, starting transfers between devices, collect_slices(): lax.all_to_all(summed.reshape(groups, capacity, width).astype(jnp.bfloat1...  28.3 us
    all_to_all x2, waiting for transfers between devices, collect_slices(): lax.all_to_all(summed.reshape(groups, capacity, width).astype(jnp.bfloat1...  10.1 us
  transfers between devices with their start and end apart: 6, of which 5 were waited for; matrix products, arithmetic and copies ran while one was open for 5% of the time, Pallas kernels for 0%

commit v1 on v0

v1 whole, which is shorter than its diff:
```python
import functools

import jax
import jax.numpy as jnp
from jax import lax
from jax.experimental import pallas as pl
from jax.experimental.pallas import tpu as pltpu
from jax.sharding import PartitionSpec as P

MESH = pl.DeviceIdType.MESH
CAP = 4
TILE = 16
LANES = 128
CHUNKS = 2
F32 = jnp.float32
BF16 = jnp.bfloat16
DIRS = (1, -1)
NT = (((1,), (1,)), ((), ()))
TN = (((0,), (0,)), ((), ()))


def dot(a, b, dims=(((1,), (0,)), ((), ()))):
    return lax.dot_general(a, b, dims, preferred_element_type=F32)


def iota(shape, axis):
    return lax.broadcasted_iota(jnp.int32, shape, axis)


def routing_matrix(ids, probs, me_e, n_e):
    toks, top = ids.shape
    shape = (toks, n_e * TILE)
    lane = iota(shape, 1)
    expert = lane // TILE + me_e
    expert = jnp.where(expert >= n_e, expert - n_e, expert)
    part = (lane % TILE) // CAP
    slot = (lane % CAP).astype(F32)
    member = jnp.zeros(shape, F32)
    weight = jnp.zeros(shape, F32)
    for k in range(top):
        same = ids[:, k : k + 1] == expert
        member = jnp.where(same, 1.0, member)
        weight = jnp.where(same, probs[:, k : k + 1], weight)
    before = (iota((toks, toks), 1) < iota((toks, toks), 0)).astype(BF16)
    count = dot(before, member.astype(BF16))
    pick = jnp.where(count == slot, member, 0.0)
    weight = pick * weight
    high = weight.astype(BF16).astype(F32)
    middle = (weight - high).astype(BF16).astype(F32)
    low = weight - high - middle
    blocks = []
    for q, value in enumerate((pick, high, middle, low)):
        for half in range(2):
            here = part == (0 if q == 0 else 2) + half
            blocks.append(jnp.where(here, value, 0.0).astype(BF16))
    return jnp.concatenate(blocks, axis=0)


def permutation(size, inverse):
    seg = size // 4
    o = iota((size, size), 1 if inverse else 0)
    i = iota((size, size), 0 if inverse else 1)
    rest = o % seg
    return (i == (rest // CAP) * TILE + (o // seg) * CAP + rest % CAP).astype(BF16)


def kernel(
    n_e, n_h, tok_ref, probs_ref, ids_ref, gate_hbm, up_hbm, down_hbm, cot_ref,
    mixed_ref, grad_ref,
    w_gu, w_down, route, send, recv, back, ret, rows, sib_out, sib_in, rs_out, rs_in, act,
    w_sem, a2a_sem, ret_sem, ag_send, ag_recv, fw_send, fw_recv, sx_send, sx_recv, rs_send, rs_recv,
):
    n_x = n_h // 2
    steps = n_x // 2
    toks, width = tok_ref.shape
    hid = gate_hbm.shape[1]
    n_rows = n_e * CAP
    piece = n_rows // CHUNKS
    group = min(16, n_e)
    me_e = lax.axis_index("expert")
    me_h = lax.axis_index("hidden")
    x = me_h // 2
    core = me_h % 2

    def at(rel, other=False):
        return ((x + (rel + n_x)) % n_x) * 2 + (1 - core if other else core)

    sibling = (me_e, x * 2 + 1 - core)

    barrier = pltpu.get_barrier_semaphore()

    def greet(j, carry):
        pl.semaphore_signal(barrier, inc=1, device_id=((me_e + j) % n_e, me_h), device_id_type=MESH)
        return carry

    lax.fori_loop(1, n_e, greet, 0)
    for d in DIRS:
        pl.semaphore_signal(barrier, inc=1, device_id=(me_e, at(d)), device_id_type=MESH)
    pl.semaphore_signal(barrier, inc=1, device_id=sibling, device_id_type=MESH)

    loads = [
        pltpu.make_async_copy(gate_hbm.at[0], w_gu.at[pl.ds(0, hid)], w_sem.at[0]),
        pltpu.make_async_copy(up_hbm.at[0], w_gu.at[pl.ds(hid, hid)], w_sem.at[1]),
        pltpu.make_async_copy(down_hbm.at[0], w_down, w_sem.at[2]),
    ]
    for load in loads:
        load.start()

    route[...] = routing_matrix(ids_ref[...], probs_ref[...], me_e, n_e)
    halves = lambda v: [v[:, :LANES], v[:, LANES:]]
    source = jnp.concatenate(halves(tok_ref[...]) + halves(cot_ref[...]) * 3, axis=0)
    send[...] = dot(route[...], source, TN).astype(BF16)

    pl.semaphore_wait(barrier, n_e + 2)

    def message(j, src, dst, sems, sign):
        place = pl.ds(pl.multiple_of(j * TILE, TILE), TILE)
        return pltpu.make_async_remote_copy(
            src_ref=src.at[place], dst_ref=dst.at[place], send_sem=sems.at[0], recv_sem=sems.at[1],
            device_id=((me_e + sign * j + n_e) % n_e, me_h), device_id_type=MESH,
        )

    def all_messages(src, dst, sems):
        place = pl.ds(TILE, (n_e - 1) * TILE)
        return pltpu.make_async_remote_copy(
            src_ref=src.at[place], dst_ref=dst.at[place], send_sem=sems.at[0], recv_sem=sems.at[1],
            device_id=((me_e + 1) % n_e, me_h), device_id_type=MESH,
        )

    def dispatch(j, carry):
        message(j, send, recv, a2a_sem, 1).start()
        return carry

    lax.fori_loop(1, n_e, dispatch, 0)
    recv[pl.ds(0, TILE)] = send[pl.ds(0, TILE)]
    order = permutation(group * TILE, False)
    all_messages(send, recv, a2a_sem).wait_recv()
    seg = group * CAP
    for g in range(n_e // group):
        sorted_rows = dot(order, recv[pl.ds(g * group * TILE, group * TILE)]).astype(BF16)
        for a in range(2):
            for half in range(2):
                q = a * 2 + half
                rows[a, me_h, pl.ds(g * seg, seg), pl.ds(half * LANES, LANES)] = sorted_rows[q * seg : (q + 1) * seg]

    def part(p):
        return pl.ds(p * piece, piece)

    def parts_of(d, k):
        if k < steps:
            return range(CHUNKS)
        return range(CHUNKS // 2) if d == 1 else range(CHUNKS // 2, CHUNKS)

    def ag(a, d, k, p, arriving=False):
        where = rows.at[a, at(-k * d if arriving else -(k - 1) * d), part(p)]
        i = 0 if d == 1 else 1
        return pltpu.make_async_remote_copy(
            src_ref=where, dst_ref=where, send_sem=ag_send.at[a, i, k - 1, p], recv_sem=ag_recv.at[a, i, k - 1, p],
            device_id=(me_e, at(d)), device_id_type=MESH,
        )

    def fw(a, rel, p, arriving=False):
        where = rows.at[a, at(rel, arriving), part(p)]
        return pltpu.make_async_remote_copy(
            src_ref=where, dst_ref=where, send_sem=fw_send.at[a, rel % n_x, p], recv_sem=fw_recv.at[a, rel % n_x, p],
            device_id=sibling, device_id_type=MESH,
        )

    def ag_begin(a):
        for p in range(CHUNKS):
            for d in DIRS:
                ag(a, d, 1, p).start()
        for p in range(CHUNKS):
            fw(a, 0, p).start()

    def ag_step(a, k):
        for p in range(CHUNKS):
            for d in DIRS:
                if p in parts_of(d, k):
                    ag(a, d, k, p, True).wait_recv()
                    if k < steps and p in parts_of(d, k + 1):
                        ag(a, d, k + 1, p).start()
                    fw(a, -k * d, p).start()

    def rels(k):
        return (0,) if k == 0 else (k,) if k == steps else (-k, k)

    def cols(h):
        return pl.ds(pl.multiple_of(h * width, width), width)

    def ag_multiply(a, k, total, weights):
        for rel in rels(k):
            for other in (False, True):
                if other:
                    for p in range(CHUNKS):
                        fw(a, rel, p, True).wait_recv()
                h = at(rel, other)
                term = dot(rows[a, h], weights[:, cols(h)], NT)
                total = term if total is None else total + term
        return total

    def own(b, rel, other):
        left = act[b, :, :hid] if b == 0 else act[b]
        right = w_down if b == 0 else w_gu
        return dot(left, right[:, cols(at(rel, other))])

    def sx(b, rel):
        i = rel % n_x
        return pltpu.make_async_remote_copy(
            src_ref=sib_out.at[b, i], dst_ref=sib_in.at[b, i], send_sem=sx_send.at[b, i], recv_sem=sx_recv.at[b, i],
            device_id=sibling, device_id_type=MESH,
        )

    far_first = [steps] + [s * k for k in range(steps - 1, 0, -1) for s in (1, -1)] + [0]

    def rs_exchange(b):
        for rel in far_first:
            sib_out[b, rel % n_x] = own(b, rel, True).astype(BF16)
            sx(b, rel).start()

    def rs(b, d, j, p):
        i = 0 if d == 1 else 1
        return pltpu.make_async_remote_copy(
            src_ref=rs_out.at[b, i, j, part(p)], dst_ref=rs_in.at[b, i, j, part(p)],
            send_sem=rs_send.at[b, i, j, p], recv_sem=rs_recv.at[b, i, j, p],
            device_id=(me_e, at(d)), device_id_type=MESH,
        )

    def rs_step(b, j):
        if j == 0:
            sx(b, steps).wait_recv()
            mine = own(b, steps, False)
            both = [mine, mine]
        else:
            both = []
            for d in DIRS:
                sx(b, (steps - j) * d).wait_recv()
                both.append(own(b, (steps - j) * d, False))
        for p in range(CHUNKS):
            for i, d in enumerate(DIRS):
                rel = steps if j == 0 else (steps - j) * d
                if p not in parts_of(d, steps - j):
                    continue
                value = both[i][p * piece : (p + 1) * piece] + sib_in[b, rel % n_x, part(p)].astype(F32)
                if j > 0 and p in parts_of(d, steps - j + 1):
                    rs(b, d, j - 1, p).wait_recv()
                    value = value + rs_in[b, i, j - 1, part(p)].astype(F32)
                rs_out[b, i, j, part(p)] = value.astype(BF16)
                rs(b, d, j, p).start()

    def rs_last(b):
        sx(b, 0).wait_recv()
        total = own(b, 0, False) + sib_in[b, 0].astype(F32)
        for i, d in enumerate(DIRS):
            for p in parts_of(d, 1):
                rs(b, d, steps - 1, p).wait_recv()
        got = [rs_in[b, i, steps - 1].astype(F32) for i in range(2)]
        return total + got[0] + got[1]

    ag_begin(0)
    for load in loads:
        load.wait()
    gate_up = ag_multiply(0, 0, None, w_gu)
    for k in range(1, steps + 1):
        ag_step(0, k)
        if k == steps - 1:
            ag_begin(1)
        gate_up = ag_multiply(0, k, gate_up, w_gu)
    gate, up = gate_up[:, :hid], gate_up[:, hid:]
    sigma = 1.0 / (1.0 + jnp.exp(-gate))
    silu = gate * sigma
    act[0, :, :hid] = (silu * up).astype(BF16)
    rs_exchange(0)
    grad_hidden = ag_multiply(1, 0, None, w_down)
    for k in range(1, steps + 1):
        ag_step(1, k)
        if k == steps:
            rs_step(0, 0)
        grad_hidden = ag_multiply(1, k, grad_hidden, w_down)
    act[1, :, :hid] = (grad_hidden * up * sigma * (1.0 + gate * (1.0 - sigma))).astype(BF16)
    act[1, :, hid:] = (grad_hidden * silu).astype(BF16)
    for j in range(1, steps):
        if j == 1:
            rs_exchange(1)
        rs_step(0, j)
    rs_step(1, 0)
    out = rs_last(0).astype(BF16)
    for j in range(1, steps):
        rs_step(1, j)
    grad = rs_last(1).astype(BF16)

    order = permutation(group * TILE, True)
    for g in range(n_e // group):
        stack = jnp.concatenate(
            [v[g * seg : (g + 1) * seg, half * LANES : (half + 1) * LANES] for v in (grad, out) for half in range(2)],
            axis=0,
        )
        back[pl.ds(g * group * TILE, group * TILE)] = dot(order, stack).astype(BF16)

    def give_back(j, carry):
        message(j, back, ret, ret_sem, -1).start()
        return carry

    lax.fori_loop(1, n_e, give_back, 0)
    ret[pl.ds(0, TILE)] = back[pl.ds(0, TILE)]
    all_messages(back, ret, ret_sem).wait_recv()
    result = dot(route[...], ret[...])
    block = lambda q, half: result[(q * 2 + half) * toks : (q * 2 + half + 1) * toks]
    for half in range(2):
        where = pl.ds(half * LANES, LANES)
        grad_ref[:, where] = block(0, half).astype(grad_ref.dtype)
        mixed_ref[:, where] = (block(1, half) + block(2, half) + block(3, half)).astype(mixed_ref.dtype)

    all_messages(send, recv, a2a_sem).wait_send()
    all_messages(back, ret, ret_sem).wait_send()
    for b in range(2):
        for d in DIRS:
            for k in range(1, steps + 1):
                for p in parts_of(d, k):
                    ag(b, d, k, p).wait_send()
                    rs(b, d, steps - k, p).wait_send()
        for rel in range(n_x):
            sx(b, rel).wait_send()
            for p in range(CHUNKS):
                fw(b, rel, p).wait_send()


def shards(tokens, probs, expert_ids, gate_weight, up_weight, down_weight, cotangent):
    n_e, n_h = lax.axis_size("expert"), lax.axis_size("hidden")
    n_x = n_h // 2
    steps = n_x // 2
    width = tokens.shape[1]
    hid, feats = gate_weight.shape[1:]
    n_rows = n_e * CAP
    dma = pltpu.SemaphoreType.DMA
    vmem = pl.BlockSpec(memory_space=pltpu.VMEM)
    hbm = pl.BlockSpec(memory_space=pl.ANY)
    messages = pltpu.VMEM((n_e * TILE, LANES), BF16)
    return pl.pallas_call(
        functools.partial(kernel, n_e, n_h),
        out_shape=(
            jax.ShapeDtypeStruct(tokens.shape, tokens.dtype),
            jax.ShapeDtypeStruct(tokens.shape, tokens.dtype),
        ),
        in_specs=[vmem, vmem, vmem, hbm, hbm, hbm, vmem],
        out_specs=(vmem, vmem),
        scratch_shapes=[
            pltpu.VMEM((2 * hid, feats), BF16),
            pltpu.VMEM((hid, feats), BF16),
            pltpu.VMEM((8 * tokens.shape[0], n_e * TILE), BF16),
            messages,
            messages,
            messages,
            messages,
            pltpu.VMEM((2, n_h, n_rows, width), BF16),
            pltpu.VMEM((2, n_x, n_rows, width), BF16),
            pltpu.VMEM((2, n_x, n_rows, width), BF16),
            pltpu.VMEM((2, 2, steps, n_rows, width), BF16),
            pltpu.VMEM((2, 2, steps, n_rows, width), BF16),
            pltpu.VMEM((2, n_rows, 2 * hid), BF16),
            dma((3,)),
            dma((2,)),
            dma((2,)),
            dma((2, 2, steps, CHUNKS)),
            dma((2, 2, steps, CHUNKS)),
            dma((2, n_x, CHUNKS)),
            dma((2, n_x, CHUNKS)),
            dma((2, n_x)),
            dma((2, n_x)),
            dma((2, 2, steps, CHUNKS)),
            dma((2, 2, steps, CHUNKS)),
        ],
        compiler_params=pltpu.CompilerParams(
            collective_id=0, has_side_effects=True, vmem_limit_bytes=48 * 1024 * 1024
        ),
    )(tokens, probs, expert_ids, gate_weight, up_weight, down_weight, cotangent)


def solution(mesh):
    placed = (
        P("expert", "hidden"),
        P("expert", None),
        P("expert", None),
        P("expert", "hidden", None),
        P("expert", "hidden", None),
        P("expert", "hidden", None),
        P("expert", "hidden"),
    )
    return jax.shard_map(
        shards,
        mesh=mesh,
        in_specs=placed,
        out_specs=(P("expert", "hidden"), P("expert", "hidden")),
        check_vma=False,
    )
```

time: 304 us -> 116 us (0.38)
  the two profiles are of different devices: /device:TPU:16 before, /device:TPU:4 now
where the time goes in v1:
time: 116 us
  Pallas kernels  109 us (94%)
  local copies, waits for them, and re-layouts  6.34 us (5%)
    pallas_call x1, Pallas kernels, shards(): pl.pallas_call(functools.partial(kernel, n_e, n_h), out_shape=(jax.ShapeD...  109 us
    unnamed x16, local copies, waits for them, and re-layouts  6.34 us

profile of v1, /device:TPU:4, one launch (start us, length us, event | category | flops | bytes accessed | tf_op | source)
XLA Modules:
  0.0 115.8 jit_solution(5577981890782524303)
XLA Ops:
  0.6 0.0 copy-start.5
  0.6 0.0 copy-start.4
  0.7 0.8 copy.9.probs_ref
  1.4 0.0 copy-done.5
  1.4 0.0 copy-start.3
  1.4 0.1 copy.10.ids_ref
  1.5 0.0 copy-done.4
  1.5 0.6 copy-done.3
  2.1 0.0 copy-start
  2.1 1.2 %copy-done = bf16[1,128,4096]{2,1,0:T(8,128)(2,1)S(1)} copy-done((bf16[1,128,4096]{2,1,0:T(8,128)(2,1)S(1)}, bf16[1,128,4096]{2,1,0:T(8,128)(2,1)}, u32[]{:S(2)}) %copy-start) | copy-done | bytes 1048600
  3.3 0.0 copy-start.1
  3.3 1.2 %copy-done.1 = bf16[1,128,4096]{2,1,0:T(8,128)(2,1)S(1)} copy-done((bf16[1,128,4096]{2,1,0:T(8,128)(2,1)S(1)}, bf16[1,128,4096]{2,1,0:T(8,128)(2,1)}, u32[]{:S(2)}) %copy-start.1) | copy-done | bytes 1048600
  4.6 0.0 copy-start.2
  4.6 1.2 %copy-done.2 = bf16[1,128,4096]{2,1,0:T(8,128)(2,1)S(1)} copy-done((bf16[1,128,4096]{2,1,0:T(8,128)(2,1)S(1)}, bf16[1,128,4096]{2,1,0:T(8,128)(2,1)}, u32[]{:S(2)}) %copy-start.2) | copy-done | bytes 1048600
  5.8 108.8 %shard_map.86 = (bf16[16,256]{1,0:T(8,128)(2,1)S(1)}, bf16[16,256]{1,0:T(8,128)(2,1)S(1)}) custom-call(bf16[16,256]{1,0:T(8,128)(2,1)S(1)} %copy-done.3, f32[16,8]{1,0:T(8,128)S(1)} %copy.9.probs_ref, s32[16,8]{1,0:T(8,128)S(1)} %copy.10.ids_ref, bf16[1,128,4096]{2,1,0:T(8,128)(2,1)S(1)} %copy-done, bf16[1,128,4096]{2,1,0:T(8,128)(2,1)S(1)} %copy-done.1, ...), custom_call_target="tpu_custom_call" | custom-call | tf_op jit(solution)/shard_map/pallas_call | solution.py:339
  114.6 0.6 copy.13
  115.2 0.6 copy.14
Async XLA Ops:
  0.6 0.8 copy-start.5
  0.6 0.9 copy-start.4
  1.4 0.7 copy-start.3
  2.1 1.2 %copy-start = (bf16[1,128,4096]{2,1,0:T(8,128)(2,1)S(1)}, bf16[1,128,4096]{2,1,0:T(8,128)(2,1)}, u32[]{:S(2)}) copy-start(bf16[1,128,4096]{2,1,0:T(8,128)(2,1)} %gate_hbm.1) | copy-start | bytes 3145732
  3.3 1.2 %copy-start.1 = (bf16[1,128,4096]{2,1,0:T(8,128)(2,1)S(1)}, bf16[1,128,4096]{2,1,0:T(8,128)(2,1)}, u32[]{:S(2)}) copy-start(bf16[1,128,4096]{2,1,0:T(8,128)(2,1)} %up_hbm.1) | copy-start | bytes 3145732
  4.6 1.2 %copy-start.2 = (bf16[1,128,4096]{2,1,0:T(8,128)(2,1)S(1)}, bf16[1,128,4096]{2,1,0:T(8,128)(2,1)}, u32[]{:S(2)}) copy-start(bf16[1,128,4096]{2,1,0:T(8,128)(2,1)} %down_hbm.1) | copy-start | bytes 3145732

commit v2 on v1

v2 whole, which is shorter than its diff:
```python
import functools

import jax
import jax.numpy as jnp
from jax import lax
from jax.experimental import pallas as pl
from jax.experimental.pallas import tpu as pltpu
from jax.sharding import PartitionSpec as P

MESH = pl.DeviceIdType.MESH
CAP = 4
TILE = 16
LANES = 128
CHUNKS = 2
F32 = jnp.float32
BF16 = jnp.bfloat16
DIRS = (1, -1)
NT = (((1,), (1,)), ((), ()))
TN = (((0,), (0,)), ((), ()))


def dot(a, b, dims=(((1,), (0,)), ((), ()))):
    return lax.dot_general(a, b, dims, preferred_element_type=F32)


def iota(shape, axis):
    return lax.broadcasted_iota(jnp.int32, shape, axis)


def routing_matrix(ids_t, probs_t, me_e, n_e):
    top, toks = ids_t.shape
    unit = (iota((top, top), 0) == iota((top, top), 1)).astype(BF16)
    turn = lambda v: dot(v.astype(BF16), unit, TN)
    ids = turn(ids_t.astype(F32)).astype(jnp.int32)
    high = probs_t.astype(BF16).astype(F32)
    middle = (probs_t - high).astype(BF16).astype(F32)
    probs = [turn(v) for v in (high, middle, probs_t - high - middle)]
    shape = (toks, n_e * TILE)
    lane = iota(shape, 1)
    expert = lane // TILE + me_e
    expert = jnp.where(expert >= n_e, expert - n_e, expert)
    part = (lane % TILE) // CAP
    slot = (lane % CAP).astype(F32)
    member = jnp.zeros(shape, F32)
    weights = [jnp.zeros(shape, F32)] * 3
    for k in range(top):
        same = ids[:, k : k + 1] == expert
        member = jnp.where(same, 1.0, member)
        weights = [jnp.where(same, v[:, k : k + 1], w) for v, w in zip(probs, weights)]
    before = (iota((toks, toks), 1) < iota((toks, toks), 0)).astype(BF16)
    count = dot(before, member.astype(BF16))
    pick = jnp.where(count == slot, member, 0.0)
    blocks = []
    for q, value in enumerate([pick] + [pick * w for w in weights]):
        for half in range(2):
            here = part == (0 if q == 0 else 2) + half
            blocks.append(jnp.where(here, value, 0.0).astype(BF16))
    return jnp.concatenate(blocks, axis=0)


def permutation(size, inverse):
    seg = size // 4
    o = iota((size, size), 1 if inverse else 0)
    i = iota((size, size), 0 if inverse else 1)
    rest = o % seg
    return (i == (rest // CAP) * TILE + (o // seg) * CAP + rest % CAP).astype(BF16)


def kernel(
    n_e, n_h, tok_hbm, probs_hbm, ids_hbm, gate_hbm, up_hbm, down_hbm, cot_hbm,
    mixed_ref, grad_ref,
    tok_ref, cot_ref, probs_ref, ids_ref,
    w_gu, w_down, route, send, recv, back, ret, send_far, recv_far, back_far, ret_far, raw, far_out, far_in, rows, sib_out, sib_in, rs_out, rs_in, act, fin, fin_far,
    w_sem, small_sem, a2a_send, a2a_recv, ret_send, ret_recv, a2a_far_send, a2a_far_recv, ret_far_send, ret_far_recv,
    cross_send, cross_recv,
    ag_send, ag_recv, fw_send, fw_recv, sx_send, sx_recv, rs_send, rs_recv,
):
    n_x = n_h // 2
    far = n_x // 2
    steps = far - 1
    toks, width = tok_ref.shape
    hid = gate_hbm.shape[1]
    piece = n_e * CAP // CHUNKS
    groups = n_e // CHUNKS
    block = min(16, groups)
    me_e = lax.axis_index("expert")
    me_h = lax.axis_index("hidden")
    x = me_h // 2
    core = me_h % 2

    def at(rel, other=False):
        return ((x + (rel + n_x)) % n_x) * 2 + (1 - core if other else core)

    sibling = (me_e, x * 2 + 1 - core)

    barrier = pltpu.get_barrier_semaphore()

    def greet(j, carry):
        pl.semaphore_signal(barrier, inc=1, device_id=((me_e + j) % n_e, me_h), device_id_type=MESH)
        return carry

    for d in DIRS:
        pl.semaphore_signal(barrier, inc=1, device_id=(me_e, at(d)), device_id_type=MESH)
    pl.semaphore_signal(barrier, inc=1, device_id=(me_e, at(far)), device_id_type=MESH)
    pl.semaphore_signal(barrier, inc=1, device_id=sibling, device_id_type=MESH)
    lax.fori_loop(1, n_e, greet, 0)

    small = [
        pltpu.make_async_copy(src, dst, small_sem.at[i])
        for i, (src, dst) in enumerate(
            ((ids_hbm, ids_ref), (probs_hbm, probs_ref), (tok_hbm, tok_ref), (cot_hbm, cot_ref))
        )
    ]
    loads = [
        pltpu.make_async_copy(gate_hbm.at[0], w_gu.at[pl.ds(0, hid)], w_sem.at[0]),
        pltpu.make_async_copy(up_hbm.at[0], w_gu.at[pl.ds(hid, hid)], w_sem.at[1]),
        pltpu.make_async_copy(down_hbm.at[0], w_down, w_sem.at[2]),
    ]
    for load in small + loads:
        load.start()
    for load in small:
        load.wait()

    route[...] = routing_matrix(ids_ref[...], probs_ref[...], me_e, n_e)
    halves = lambda v: [v[:, :LANES], v[:, LANES:]]

    def placed(tok, cot):
        source = jnp.concatenate(halves(tok) + halves(cot) * 3, axis=0)
        return dot(route[...], source, TN).astype(BF16)

    send[...] = placed(tok_ref[...], cot_ref[...])
    for load in loads:
        load.wait()

    pl.semaphore_wait(barrier, n_e + 3)

    def message(j, p, src, dst, sems, sign):
        place = pl.ds(pl.multiple_of(j * TILE, TILE), TILE)
        return pltpu.make_async_remote_copy(
            src_ref=src.at[place], dst_ref=dst.at[place], send_sem=sems[0].at[p], recv_sem=sems[1].at[p],
            device_id=((me_e + sign * j + n_e) % n_e, me_h), device_id_type=MESH,
        )

    def first(p):
        return 1 if p == 0 else p * groups

    def post(p, src, dst, sems, sign):
        def one(j, carry):
            message(j, p, src, dst, sems, sign).start()
            return carry

        lax.fori_loop(first(p), (p + 1) * groups, one, 0)

    def posted(p, src, dst, sems):
        place = pl.ds(first(p) * TILE, ((p + 1) * groups - first(p)) * TILE)
        return pltpu.make_async_remote_copy(
            src_ref=src.at[place], dst_ref=dst.at[place], send_sem=sems[0].at[p], recv_sem=sems[1].at[p],
            device_id=((me_e + 1) % n_e, me_h), device_id_type=MESH,
        )

    out_way = (send, recv, (a2a_send, a2a_recv))
    home_way = (back, ret, (ret_send, ret_recv))
    out_far = (send_far, recv_far, (a2a_far_send, a2a_far_recv))
    home_far = (back_far, ret_far, (ret_far_send, ret_far_recv))

    def cross(i, src, dst):
        return pltpu.make_async_remote_copy(
            src_ref=src, dst_ref=dst, send_sem=cross_send.at[i], recv_sem=cross_recv.at[i],
            device_id=(me_e, at(far)), device_id_type=MESH,
        )

    crossing = [cross(0, tok_ref, raw.at[0]), cross(1, cot_ref, raw.at[1]), cross(2, far_out, far_in)]

    def part(p):
        return pl.ds(p * piece, piece)

    seg = block * CAP
    order = permutation(block * TILE, False)

    def arrive(p, way, rel):
        posted(p, *way).wait_recv()
        for g in range(p * groups // block, (p + 1) * groups // block):
            sorted_rows = dot(order, way[1][pl.ds(g * block * TILE, block * TILE)]).astype(BF16)
            for a in range(2):
                for half in range(2):
                    q = a * 2 + half
                    rows[a, at(rel), pl.ds(g * seg, seg), pl.ds(half * LANES, LANES)] = sorted_rows[q * seg : (q + 1) * seg]

    def ag(a, p, d, k, arriving=False):
        where = rows.at[a, at(-k * d if arriving else -(k - 1) * d), part(p)]
        i = 0 if d == 1 else 1
        return pltpu.make_async_remote_copy(
            src_ref=where, dst_ref=where, send_sem=ag_send.at[a, i, k - 1, p], recv_sem=ag_recv.at[a, i, k - 1, p],
            device_id=(me_e, at(d)), device_id_type=MESH,
        )

    def fw(a, p, rel, arriving=False):
        where = rows.at[a, at(rel, arriving), part(p)]
        return pltpu.make_async_remote_copy(
            src_ref=where, dst_ref=where, send_sem=fw_send.at[a, rel % n_x, p], recv_sem=fw_recv.at[a, rel % n_x, p],
            device_id=sibling, device_id_type=MESH,
        )

    def gather(a, p, k):
        for d in DIRS:
            if k:
                ag(a, p, d, k, True).wait_recv()
            if k < steps:
                ag(a, p, d, k + 1).start()
            if k:
                fw(a, p, -k * d).start()
        if not k:
            fw(a, p, 0).start()

    def gather_far(p):
        arrive(p, out_far, far)
        for a in range(2):
            fw(a, p, far).start()

    def cols(h):
        return pl.ds(pl.multiple_of(h * width, width), width)

    sums = {}

    def multiply(a, p, k):
        weights = w_down if a else w_gu
        for rel in (-k, k) if 0 < k < far else (k,):
            for other in (False, True):
                if other:
                    fw(a, p, rel, True).wait_recv()
                h = at(rel, other)
                term = dot(rows[a, h, part(p)], weights[:, cols(h)], NT)
                sums[a, p] = sums[a, p] + term if (a, p) in sums else term

    def own(b, p, rel, other):
        left = act[b, part(p)] if b else act[b, part(p), :hid]
        right = w_gu if b else w_down
        return dot(left, right[:, cols(at(rel, other))])

    def sx(b, p, rel):
        i = rel % n_x
        return pltpu.make_async_remote_copy(
            src_ref=sib_out.at[b, i, part(p)], dst_ref=sib_in.at[b, i, part(p)],
            send_sem=sx_send.at[b, i, p], recv_sem=sx_recv.at[b, i, p],
            device_id=sibling, device_id_type=MESH,
        )

    def exchange(b, p, k):
        for rel in (k, -k) if 0 < k < far else (k,):
            sib_out[b, rel % n_x, part(p)] = own(b, p, rel, True).astype(BF16)
            sx(b, p, rel).start()

    def forward_act(p):
        gate, up = sums[0, p][:, :hid], sums[0, p][:, hid:]
        sigma = 1.0 / (1.0 + jnp.exp(-gate))
        act[0, part(p), :hid] = (gate * sigma * up).astype(BF16)
        exchange(0, p, steps)

    def backward_act(p):
        gate, up = sums[0, p][:, :hid], sums[0, p][:, hid:]
        sigma = 1.0 / (1.0 + jnp.exp(-gate))
        act[1, part(p), :hid] = (sums[1, p] * up * sigma * (1.0 + gate * (1.0 - sigma))).astype(BF16)
        act[1, part(p), hid:] = (sums[1, p] * gate * sigma).astype(BF16)
        exchange(1, p, steps)

    def rs(b, p, d, j):
        i = 0 if d == 1 else 1
        return pltpu.make_async_remote_copy(
            src_ref=rs_out.at[b, i, j, part(p)], dst_ref=rs_in.at[b, i, j, part(p)],
            send_sem=rs_send.at[b, i, j, p], recv_sem=rs_recv.at[b, i, j, p],
            device_id=(me_e, at(d)), device_id_type=MESH,
        )

    def pair_sum(b, p, rel):
        value = own(b, p, rel, False)
        sx(b, p, rel).wait_recv()
        return value + sib_in[b, rel % n_x, part(p)].astype(F32)

    def reduce(b, p, j):
        for i, d in enumerate(DIRS):
            value = pair_sum(b, p, (steps - j) * d)
            if j > 0:
                rs(b, p, d, j - 1).wait_recv()
                value = value + rs_in[b, i, j - 1, part(p)].astype(F32)
            rs_out[b, i, j, part(p)] = value.astype(BF16)
            rs(b, p, d, j).start()

    def finish(b, p):
        value = pair_sum(b, p, 0)
        for i, d in enumerate(DIRS):
            rs(b, p, d, steps - 1).wait_recv()
            value = value + rs_in[b, i, steps - 1, part(p)].astype(F32)
        fin[b, part(p)] = value.astype(BF16)

    def finish_far(p):
        for b in range(2):
            fin_far[b, part(p)] = pair_sum(b, p, far).astype(BF16)
        give_back(p, fin_far, home_far)

    inverse = permutation(block * TILE, True)

    def give_back(p, whole, way):
        for g in range(p * groups // block, (p + 1) * groups // block):
            stack = jnp.concatenate(
                [whole[b, pl.ds(g * seg, seg), pl.ds(half * LANES, LANES)] for b in (1, 0) for half in range(2)], axis=0
            )
            way[0][pl.ds(g * block * TILE, block * TILE)] = dot(inverse, stack).astype(BF16)
        post(p, *way, -1)
        if p == 0:
            way[1][pl.ds(0, TILE)] = way[0][pl.ds(0, TILE)]

    crossing[0].start()
    crossing[1].start()
    for p in range(CHUNKS):
        post(p, *out_way, 1)
    recv[pl.ds(0, TILE)] = send[pl.ds(0, TILE)]
    crossing[0].wait_recv()
    crossing[1].wait_recv()
    send_far[...] = placed(raw[0], raw[1])
    recv_far[pl.ds(0, TILE)] = send_far[pl.ds(0, TILE)]
    late = []
    for p in range(CHUNKS):
        arrive(p, out_way, 0)
        for a in range(2):
            gather(a, p, 0)
            late.append((a, p, 0))
        post(p, *out_far, 1)
    units = list(late)
    for k in range(1, steps + 1):
        for a, p, _ in units:
            gather(a, p, k)
            if k == max(1, steps - 1) and a == 1:
                gather_far(p)
                late += [(0, p, far), (1, p, far)]
            for unit in late[:2]:
                multiply(*unit)
            late = late[2:] + [(a, p, k)]
    todo = []
    for a, p, _ in units:
        for unit in [u for u in late if u[:2] == (a, p)]:
            multiply(*unit)
        (backward_act if a else forward_act)(p)
        for unit in todo:
            reduce(*unit)
        todo = [(a, p, 0)]
    for unit in todo:
        reduce(*unit)
    for j in range(1, steps):
        for b, p, _ in units:
            exchange(b, p, steps - j)
            reduce(b, p, j)
        for b, p, _ in units:
            if j == 1:
                exchange(b, p, far)
    if steps < 2:
        for b, p, _ in units:
            exchange(b, p, far)
    for p in range(CHUNKS):
        finish_far(p)
    for b, p, _ in units:
        exchange(b, p, 0)
    for b, p, _ in units:
        finish(b, p)
        if b:
            give_back(p, fin, home_way)

    def combine(way):
        total = None
        for p in range(CHUNKS):
            posted(p, *way).wait_recv()
            place = pl.ds(p * groups * TILE, groups * TILE)
            term = dot(route[:, place], way[1][place])
            total = term if total is None else total + term
        rows_of = lambda q, half: total[(q * 2 + half) * toks : (q * 2 + half + 1) * toks]
        grad = [rows_of(0, half) for half in range(2)]
        return grad, [rows_of(1, half) + rows_of(2, half) + rows_of(3, half) for half in range(2)]

    for i, pair in enumerate(combine(home_far)):
        for half in range(2):
            far_out[pl.ds(i * toks, toks), pl.ds(half * LANES, LANES)] = pair[half]
    crossing[2].start()
    near = combine(home_way)
    crossing[2].wait_recv()
    for i, (pair, out) in enumerate(zip(near, (grad_ref, mixed_ref))):
        for half in range(2):
            where = pl.ds(half * LANES, LANES)
            out[:, where] = (pair[half] + far_in[pl.ds(i * toks, toks), where]).astype(out.dtype)

    for copy in crossing:
        copy.wait_send()
    for p in range(CHUNKS):
        for way in (out_way, home_way, out_far, home_far):
            posted(p, *way).wait_send()
        for b in range(2):
            for k in range(1, steps + 1):
                for d in DIRS:
                    ag(b, p, d, k).wait_send()
                    rs(b, p, d, steps - k).wait_send()
            for rel in range(n_x):
                sx(b, p, rel).wait_send()
                fw(b, p, rel).wait_send()


def shards(tokens, probs, expert_ids, gate_weight, up_weight, down_weight, cotangent):
    n_e, n_h = lax.axis_size("expert"), lax.axis_size("hidden")
    n_x = n_h // 2
    steps = n_x // 2 - 1
    width = tokens.shape[1]
    hid, feats = gate_weight.shape[1:]
    n_rows = n_e * CAP
    dma = pltpu.SemaphoreType.DMA
    vmem = pl.BlockSpec(memory_space=pltpu.VMEM)
    hbm = pl.BlockSpec(memory_space=pltpu.HBM)
    messages = pltpu.VMEM((n_e * TILE, LANES), BF16)
    return pl.pallas_call(
        functools.partial(kernel, n_e, n_h),
        out_shape=(
            jax.ShapeDtypeStruct(tokens.shape, tokens.dtype),
            jax.ShapeDtypeStruct(tokens.shape, tokens.dtype),
        ),
        in_specs=[hbm] * 7,
        out_specs=(vmem, vmem),
        scratch_shapes=[
            pltpu.VMEM(tokens.shape, BF16),
            pltpu.VMEM(tokens.shape, BF16),
            pltpu.VMEM(probs.shape[::-1], F32),
            pltpu.VMEM(probs.shape[::-1], jnp.int32),
            pltpu.VMEM((2 * hid, feats), BF16),
            pltpu.VMEM((hid, feats), BF16),
            pltpu.VMEM((8 * tokens.shape[0], n_e * TILE), BF16),
            *[messages] * 8,
            pltpu.VMEM((2, *tokens.shape), BF16),
            pltpu.VMEM((2 * tokens.shape[0], width), F32),
            pltpu.VMEM((2 * tokens.shape[0], width), F32),
            pltpu.VMEM((2, n_h, n_rows, width), BF16),
            pltpu.VMEM((2, n_x, n_rows, width), BF16),
            pltpu.VMEM((2, n_x, n_rows, width), BF16),
            pltpu.VMEM((2, 2, steps, n_rows, width), BF16),
            pltpu.VMEM((2, 2, steps, n_rows, width), BF16),
            pltpu.VMEM((2, n_rows, 2 * hid), BF16),
            pltpu.VMEM((2, n_rows, width), BF16),
            pltpu.VMEM((2, n_rows, width), BF16),
            dma((3,)),
            dma((4,)),
            *[dma((CHUNKS,))] * 8,
            dma((3,)),
            dma((3,)),
            dma((2, 2, steps, CHUNKS)),
            dma((2, 2, steps, CHUNKS)),
            dma((2, n_x, CHUNKS)),
            dma((2, n_x, CHUNKS)),
            dma((2, n_x, CHUNKS)),
            dma((2, n_x, CHUNKS)),
            dma((2, 2, steps, CHUNKS)),
            dma((2, 2, steps, CHUNKS)),
        ],
        compiler_params=pltpu.CompilerParams(
            collective_id=0, has_side_effects=True, vmem_limit_bytes=63 * 1024 * 1024
        ),
    )(tokens, probs.T, expert_ids.T, gate_weight, up_weight, down_weight, cotangent)


def solution(mesh):
    placed = (
        P("expert", "hidden"),
        P("expert", None),
        P("expert", None),
        P("expert", "hidden", None),
        P("expert", "hidden", None),
        P("expert", "hidden", None),
        P("expert", "hidden"),
    )
    return jax.shard_map(
        shards,
        mesh=mesh,
        in_specs=placed,
        out_specs=(P("expert", "hidden"), P("expert", "hidden")),
        check_vma=False,
    )
```

time: 116 us -> 95 us (0.82)
  the two profiles are of different devices: /device:TPU:4 before, /device:TPU:16 now
where the time goes in v2:
time: 95 us; the launch traced here: 94.8 us
  Pallas kernels  92.2 us (97%)
  local copies, waits for them, and re-layouts  1.9 us (2%)
    pallas_call x1, Pallas kernels, shards(): pl.pallas_call(functools.partial(kernel, n_e, n_h), out_shape=(jax.ShapeD...  92.2 us
    unnamed x4, local copies, waits for them, and re-layouts  1.9 us

profile of v2, /device:TPU:16, one launch (start us, length us, event | category | flops | bytes accessed | tf_op | source)
XLA Modules:
  0.0 94.8 jit_solution(7964755165166108728)
XLA Ops:
  0.6 92.2 %shard_map.86 = (bf16[16,256]{1,0:T(8,128)(2,1)}, bf16[16,256]{1,0:T(8,128)(2,1)}) custom-call(bf16[16,256]{1,0:T(8,128)(2,1)} %tok_hbm.1, f32[8,16]{1,0:T(8,128)} %bitcast.2, s32[8,16]{1,0:T(8,128)} %bitcast.3, bf16[1,128,4096]{2,1,0:T(8,128)(2,1)} %gate_hbm.1, bf16[1,128,4096]{2,1,0:T(8,128)(2,1)} %up_hbm.1, bf16[1,128,4096]{2,1,0:T(8,128)(2,1)} %down_hbm.1, ...), custom_call_target="tpu_custom_call" | custom-call | tf_op jit(solution)/shard_map/pallas_call | solution.py:415
  92.9 0.0 copy-start
  92.9 1.3 %copy.11 = bf16[16,256]{1,0:T(8,128)(2,1)} copy(bf16[16,256]{1,0:T(8,128)(2,1)} %get-tuple-element.4) | data formatting | bytes 16384
  94.2 0.0 copy-done
  94.2 0.6 copy.12
Async XLA Ops:
  92.9 1.3 %copy-start = (bf16[16,256]{1,0:T(8,128)(2,1)S(1)}, bf16[16,256]{1,0:T(8,128)(2,1)}, u32[]{:S(2)}) copy-start(bf16[16,256]{1,0:T(8,128)(2,1)} %get-tuple-element.5) | copy-start | bytes 24580

commit v3 on v2

--- a/solution.py
+++ b/solution.py
@@ -1,4 +1,5 @@
 import functools
+import math
 
 import jax
 import jax.numpy as jnp
@@ -27,6 +28,11 @@
     return lax.broadcasted_iota(jnp.int32, shape, axis)
 
 
+def torus(n_e):
+    rows = math.isqrt(n_e)
+    return rows, n_e // rows, (0, 1, 7, 4, 2, 6, 3, 5) if rows == 8 else tuple(range(rows))
+
+
 def routing_matrix(ids_t, probs_t, me_e, n_e):
     top, toks = ids_t.shape
     unit = (iota((top, top), 0) == iota((top, top), 1)).astype(BF16)
@@ -37,8 +43,12 @@
     probs = [turn(v) for v in (high, middle, probs_t - high - middle)]
     shape = (toks, n_e * TILE)
     lane = iota(shape, 1)
-    expert = lane // TILE + me_e
-    expert = jnp.where(expert >= n_e, expert - n_e, expert)
+    n_y, n_z, order = torus(n_e)
+    place = lane // TILE
+    y = jnp.zeros(shape, jnp.int32)
+    for i, dy in enumerate(order):
+        y = jnp.where(place // n_z == i, (me_e // n_z + dy) % n_y, y)
+    expert = y * n_z + (place % n_z + me_e) % n_z
     part = (lane % TILE) // CAP
     slot = (lane % CAP).astype(F32)
     member = jnp.zeros(shape, F32)
@@ -134,22 +144,32 @@
 
     pl.semaphore_wait(barrier, n_e + 3)
 
-    def message(j, p, src, dst, sems, sign):
-        place = pl.ds(pl.multiple_of(j * TILE, TILE), TILE)
+    n_y, n_z, turns = torus(n_e)
+
+    def message(i, dz, p, src, dst, sems, sign):
+        place = pl.ds(pl.multiple_of((i * n_z + dz) * TILE, TILE), TILE)
+        y = (me_e // n_z + sign * turns[i] + n_y) % n_y
+        z = (me_e % n_z + sign * dz + n_z) % n_z
         return pltpu.make_async_remote_copy(
             src_ref=src.at[place], dst_ref=dst.at[place], send_sem=sems[0].at[p], recv_sem=sems[1].at[p],
-            device_id=((me_e + sign * j + n_e) % n_e, me_h), device_id_type=MESH,
+            device_id=(y * n_z + z, me_h), device_id_type=MESH,
         )
 
     def first(p):
         return 1 if p == 0 else p * groups
 
     def post(p, src, dst, sems, sign):
-        def one(j, carry):
-            message(j, p, src, dst, sems, sign).start()
+        per = groups // n_z
+
+        def some(dz, carry):
+            for i in range(p * per, (p + 1) * per):
+                message(i, dz, p, src, dst, sems, sign).start()
             return carry
 
-        lax.fori_loop(first(p), (p + 1) * groups, one, 0)
+        if p == 0:
+            for i in range(1, per):
+                message(i, 0, p, src, dst, sems, sign).start()
+        lax.fori_loop(0 if p else 1, n_z, some, 0)
 
     def posted(p, src, dst, sems):
         place = pl.ds(first(p) * TILE, ((p + 1) * groups - first(p)) * TILE)
@@ -277,8 +297,8 @@
         return value + sib_in[b, rel % n_x, part(p)].astype(F32)
 
     def reduce(b, p, j):
-        for i, d in enumerate(DIRS):
-            value = pair_sum(b, p, (steps - j) * d)
+        values = [pair_sum(b, p, (steps - j) * d) for d in DIRS]
+        for i, (d, value) in enumerate(zip(DIRS, values)):
             if j > 0:
                 rs(b, p, d, j - 1).wait_recv()
                 value = value + rs_in[b, i, j - 1, part(p)].astype(F32)
@@ -324,41 +344,51 @@
         for a in range(2):
             gather(a, p, 0)
             late.append((a, p, 0))
-        post(p, *out_far, 1)
     units = list(late)
+    post(0, *out_far, 1)
+    ready = []
+
+    def start_sums(unit):
+        for one in [u for u in late if u[:2] == unit]:
+            late.remove(one)
+            multiply(*one)
+        (backward_act if unit[0] else forward_act)(unit[1])
+        ready.append(unit)
+        if len(ready) > 1:
+            first_sums(ready[-2])
+
+    def first_sums(unit):
+        reduce(*unit, 0)
+        exchange(*unit, steps - 1)
+
     for k in range(1, steps + 1):
-        for a, p, _ in units:
+        for n, (a, p, _) in enumerate(units):
             gather(a, p, k)
-            if k == max(1, steps - 1) and a == 1:
+            if k == 1 and n == 1:
+                for q in range(1, CHUNKS):
+                    post(q, *out_far, 1)
+            if k == steps and n > 0:
+                start_sums(units[n - 1][:2])
+            for unit in late[:2]:
+                multiply(*unit)
+            del late[:2]
+            late.append((a, p, k))
+            if k == steps - 1 and a == 1:
                 gather_far(p)
                 late += [(0, p, far), (1, p, far)]
-            for unit in late[:2]:
-                multiply(*unit)
-            late = late[2:] + [(a, p, k)]
-    todo = []
-    for a, p, _ in units:
-        for unit in [u for u in late if u[:2] == (a, p)]:
-            multiply(*unit)
-        (backward_act if a else forward_act)(p)
-        for unit in todo:
-            reduce(*unit)
-        todo = [(a, p, 0)]
-    for unit in todo:
-        reduce(*unit)
+    start_sums(units[-1][:2])
+    first_sums(units[-1][:2])
+    for b, p, _ in units:
+        exchange(b, p, far)
     for j in range(1, steps):
         for b, p, _ in units:
-            exchange(b, p, steps - j)
             reduce(b, p, j)
-        for b, p, _ in units:
+            if j < steps - 1:
+                exchange(b, p, steps - 1 - j)
             if j == 1:
-                exchange(b, p, far)
-    if steps < 2:
-        for b, p, _ in units:
-            exchange(b, p, far)
-    for p in range(CHUNKS):
-        finish_far(p)
-    for b, p, _ in units:
-        exchange(b, p, 0)
+                exchange(b, p, 0)
+                if b:
+                    finish_far(p)
     for b, p, _ in units:
         finish(b, p)
         if b:

time: 95 us -> 84.7 us (0.89)
  the two profiles are of different devices: /device:TPU:16 before, /device:TPU:6 now
where the time goes in v3:
time: 84.7 us; the launch traced here: 84.5 us
  Pallas kernels  82 us (97%)
  local copies, waits for them, and re-layouts  1.9 us (2%)
    pallas_call x1, Pallas kernels, shards(): pl.pallas_call(functools.partial(kernel, n_e, n_h), out_shape=(jax.ShapeD...  82 us
    unnamed x4, local copies, waits for them, and re-layouts  1.9 us

profile of v3, /device:TPU:6, one launch (start us, length us, event | category | flops | bytes accessed | tf_op | source)
XLA Modules:
  0.0 84.5 jit_solution(8130334543883920851)
XLA Ops:
  0.6 82.0 %shard_map.86 = (bf16[16,256]{1,0:T(8,128)(2,1)}, bf16[16,256]{1,0:T(8,128)(2,1)}) custom-call(bf16[16,256]{1,0:T(8,128)(2,1)} %tok_hbm.1, f32[8,16]{1,0:T(8,128)} %bitcast.2, s32[8,16]{1,0:T(8,128)} %bitcast.3, bf16[1,128,4096]{2,1,0:T(8,128)(2,1)} %gate_hbm.1, bf16[1,128,4096]{2,1,0:T(8,128)(2,1)} %up_hbm.1, bf16[1,128,4096]{2,1,0:T(8,128)(2,1)} %down_hbm.1, ...), custom_call_target="tpu_custom_call" | custom-call | tf_op jit(solution)/shard_map/pallas_call | solution.py:445
  82.6 0.0 copy-start
  82.6 1.3 %copy.11 = bf16[16,256]{1,0:T(8,128)(2,1)} copy(bf16[16,256]{1,0:T(8,128)(2,1)} %get-tuple-element.4) | data formatting | bytes 16384
  83.9 0.0 copy-done
  84.0 0.6 copy.12
Async XLA Ops:
  82.6 1.3 %copy-start = (bf16[16,256]{1,0:T(8,128)(2,1)S(1)}, bf16[16,256]{1,0:T(8,128)(2,1)}, u32[]{:S(2)}) copy-start(bf16[16,256]{1,0:T(8,128)(2,1)} %get-tuple-element.5) | copy-start | bytes 24580

commit v4 on v3

--- a/solution.py
+++ b/solution.py
@@ -161,15 +161,17 @@
     def post(p, src, dst, sems, sign):
         per = groups // n_z
 
-        def some(dz, carry):
-            for i in range(p * per, (p + 1) * per):
+        def some(turn, carry):
+            near = n_z - 1 - turn
+            dz = (near % 2 * ((near + 1) // 2) + (1 - near % 2) * (n_z - near // 2)) % n_z
+            for i in reversed(range(p * per, (p + 1) * per)):
                 message(i, dz, p, src, dst, sems, sign).start()
             return carry
 
         if p == 0:
             for i in range(1, per):
                 message(i, 0, p, src, dst, sems, sign).start()
-        lax.fori_loop(0 if p else 1, n_z, some, 0)
+        lax.fori_loop(0, n_z if p else n_z - 1, some, 0)
 
     def posted(p, src, dst, sems):
         place = pl.ds(first(p) * TILE, ((p + 1) * groups - first(p)) * TILE)
@@ -227,10 +229,8 @@
                 ag(a, p, d, k, True).wait_recv()
             if k < steps:
                 ag(a, p, d, k + 1).start()
-            if k:
-                fw(a, p, -k * d).start()
-        if not k:
-            fw(a, p, 0).start()
+        for rel in (-k, k) if k else (0,):
+            fw(a, p, rel).start()
 
     def gather_far(p):
         arrive(p, out_far, far)

time: 84.7 us -> 84.3 us (level)
  the two profiles are of different devices: /device:TPU:6 before, /device:TPU:4 now
where the time goes in v4:
time: 84.3 us; the launch traced here: 84.1 us
  Pallas kernels  81.5 us (97%)
  local copies, waits for them, and re-layouts  1.9 us (2%)
    pallas_call x1, Pallas kernels, shards(): pl.pallas_call(functools.partial(kernel, n_e, n_h), out_shape=(jax.ShapeD...  81.5 us
    unnamed x4, local copies, waits for them, and re-layouts  1.9 us

profile of v4, /device:TPU:4, one launch (start us, length us, event | category | flops | bytes accessed | tf_op | source)
XLA Modules:
  0.0 84.1 jit_solution(14188227102965224956)
XLA Ops:
  0.6 81.5 %shard_map.86 = (bf16[16,256]{1,0:T(8,128)(2,1)}, bf16[16,256]{1,0:T(8,128)(2,1)}) custom-call(bf16[16,256]{1,0:T(8,128)(2,1)} %tok_hbm.1, f32[8,16]{1,0:T(8,128)} %bitcast.2, s32[8,16]{1,0:T(8,128)} %bitcast.3, bf16[1,128,4096]{2,1,0:T(8,128)(2,1)} %gate_hbm.1, bf16[1,128,4096]{2,1,0:T(8,128)(2,1)} %up_hbm.1, bf16[1,128,4096]{2,1,0:T(8,128)(2,1)} %down_hbm.1, ...), custom_call_target="tpu_custom_call" | custom-call | tf_op jit(solution)/shard_map/pallas_call | solution.py:445
  82.2 0.0 copy-start
  82.2 1.3 %copy.11 = bf16[16,256]{1,0:T(8,128)(2,1)} copy(bf16[16,256]{1,0:T(8,128)(2,1)} %get-tuple-element.4) | data formatting | bytes 16384
  83.5 0.0 copy-done
  83.5 0.6 copy.12
Async XLA Ops:
  82.2 1.3 %copy-start = (bf16[16,256]{1,0:T(8,128)(2,1)S(1)}, bf16[16,256]{1,0:T(8,128)(2,1)}, u32[]{:S(2)}) copy-start(bf16[16,256]{1,0:T(8,128)(2,1)} %get-tuple-element.5) | copy-start | bytes 24580
